TPU v7x, 256 devices: a whole 4x4x8 slice. The times are simulated.
256 devices in a mesh: req: 8 (over y, core), kv: 32 (over z, x).
Axes of the slice: x: 4, y: 4, z: 8, core: 2. Of those that a mesh axis runs over, the one named last changes fastest.
Arguments:
- q_nope: bfloat16 [32, 128, 128], P('req', 'kv'), may hold values from -6 to 6
- q_rope: bfloat16 [32, 128, 64], P('req', 'kv'), may hold values from -8 to 8
- cache: bfloat16 [32, 65536, 576], P('req', 'kv'), may hold values from -14 to 14
- lengths: int32 [32], P('req'), may hold values from 2 to 65536, as said below
- w_uk: bfloat16 [128, 128, 512], P('kv'), may hold values from -0.5 to 0.5
- w_uv: bfloat16 [128, 512, 128], P('kv'), may hold values from -0.25 to 0.25
Outputs:
- attn: bfloat16 [32, 16384], P('req', 'kv')
Inputs may be any that keep to these rules, and one draw needn't show every extreme that they name: `lengths`: some request has exactly 65536.
All inputs are finite; a program needn't handle non-finite values.
Results may differ from a plain program's by a relative error of at most 0.0084.
Values may be sent and summed in bfloat16 or wider, within the bound.
A program may use at most 128 MiB of HBM per device.

v0:
```python
import jax
import jax.numpy as jnp
from jax import lax
from jax.sharding import PartitionSpec as P


def local(q_nope, q_rope, cache, lengths, w_uk, w_uv):
    heads_dev = q_nope.shape[1]
    latent_width = w_uk.shape[2]
    split_len = cache.shape[1]
    score_scale = (q_nope.shape[2] + q_rope.shape[2]) ** (-0.5)
    q_lat = jnp.einsum("bhd,hdc->bhc", q_nope, w_uk, preferred_element_type=jnp.float32).astype(
        jnp.bfloat16
    )
    query_full = jnp.concatenate([q_lat, q_rope], axis=2)
    queries_all = lax.all_gather(query_full, "kv", axis=1, tiled=True)
    scores = (
        jnp.einsum("bhk,btk->bht", queries_all, cache, preferred_element_type=jnp.float32)
        * score_scale
    )
    positions = lax.axis_index("kv") * split_len + jnp.arange(split_len, dtype=jnp.int32)
    is_live = positions[None, None, :] < lengths[:, None, None]
    scores = jnp.where(is_live, scores, jnp.float32(-1e30))
    top_local = jnp.max(scores, axis=2)
    weights = jnp.where(is_live, jnp.exp(scores - top_local[:, :, None]), jnp.float32(0.0))
    local_sum = jnp.sum(weights, axis=2)
    local_out = jnp.einsum(
        "bht,btc->bhc",
        weights.astype(jnp.bfloat16),
        cache[:, :, :latent_width],
        preferred_element_type=jnp.float32,
    )
    head_start = lax.axis_index("kv") * heads_dev
    top_score = lax.pmax(top_local, "kv")
    factor = jnp.exp(top_local - top_score)
    summed_out, summed_den = lax.psum((local_out * factor[:, :, None], local_sum * factor), "kv")
    numerator = lax.dynamic_slice_in_dim(summed_out, head_start, heads_dev, 1)
    denominator = lax.dynamic_slice_in_dim(summed_den, head_start, heads_dev, 1)
    latent_out = (numerator / denominator[:, :, None]).astype(jnp.bfloat16)
    attn = jnp.einsum("bhc,hcv->bhv", latent_out, w_uv, preferred_element_type=jnp.float32).astype(
        jnp.bfloat16
    )
    return attn.reshape(attn.shape[0], heads_dev * attn.shape[2])


def solution(mesh):
    in_specs = (
        P("req", "kv", None),
        P("req", "kv", None),
        P("req", "kv", None),
        P("req"),
        P("kv", None, None),
        P("kv", None, None),
    )
    out_specs = P("req", "kv")
    return jax.shard_map(local, mesh=mesh, in_specs=in_specs, out_specs=out_specs, check_vma=False)
```

profile of v0, /device:TPU:8, one launch (start us, length us, event | category | flops | bytes accessed | tf_op | source)
XLA Modules:
  0.0 302.3 jit_solution(17117205833248305423)
XLA Ops:
  6.5 0.0 copy-start
  6.5 0.0 all-reduce.2.cloned.1.call-start
  6.5 0.7 copy.9
  7.3 0.3 copy-done
  7.6 0.9 fusion.11
  8.5 52.9 %all_gather.3 = bf16[4,128,576]{2,0,1:T(4,128)(2,1)S(1)} all-gather(bf16[4,4,576]{2,0,1:T(4,128)(2,1)S(1)} %pad_maximum_fusion), channel_id=1, replica_groups=mesh['req'=8,'kv'=32] {'kv'}, dimensions={1}, use_global_device_ids=true | all-gather | bytes 608256 | tf_op jit(solution)/shard_map/all_gather | solution.py:16
  61.4 0.9 broadcast_compare_fusion
  62.3 0.0 slice-start.1
  62.3 0.0 slice-start.2
  62.3 6.3 %fusion.2 = (f32[4,128]{1,0:T(4,128)S(1)}, f32[4,128,2048]{2,1,0:T(8,128)S(1)}) fusion(pred[4,2048]{1,0:T(4,128)(4,1)S(1)} %broadcast_compare_fusion, bf16[4,2048,576]{1,2,0:T(8,128)(2,1)} %param.8, bf16[4,128,576]{2,0,1:T(4,128)(2,1)S(1)} %all_gather.3), kind=kOutput, calls=%fused_computation.4 | convolution fusion | flops 1211104768 | bytes 14231552 | tf_op jit(solution)/shard_map/bhk,btk->bht/dot_general | solution.py:18
  68.7 1.2 fusion.3
  69.9 0.0 slice-done
  69.9 0.0 slice-done.1
  69.9 0.0 copy-start.1
  69.9 3.5 %fusion = f32[4,128,512]{2,1,0:T(8,128)S(1)} fusion(bf16[4,2048,576]{1,2,0:T(8,128)(2,1)S(1)} %bitcast.10, f32[4,128,2048]{2,1,0:T(8,128)S(1)} %get-tuple-element.8, f32[4,128]{1,0:T(4,128)S(1)} %get-tuple-element.7, pred[4,2048]{1,0:T(4,128)(4,1)S(1)} %broadcast_compare_fusion), kind=kOutput, calls=%fused_computation | convolution fusion | flops 1078984704 | bytes 13641728 | tf_op jit(solution)/shard_map/bht,btc->bhc/dot_general | solution.py:27
  73.4 72.3 %pmax.7 = f32[4,128]{1,0:T(4,128)S(1)} all-reduce(f32[4,128]{1,0:T(4,128)S(1)} %get-tuple-element.7), channel_id=1, replica_groups=mesh['req'=8,'kv'=32] {'kv'}, use_global_device_ids=true, to_apply=%region_1.2 | all-reduce | flops 512 | bytes 4096 | tf_op jit(solution)/shard_map/pmax | solution.py:34
  145.7 0.1 copy.11
  145.8 1.8 copy_multiply_fusion
  147.6 0.0 all-reduce.2.cloned.1.call-update
  147.6 69.7 %psum.15 = f32[4,128]{1,0:T(4,128)S(1)} all-reduce(f32[4,128]{1,0:T(4,128)S(1)} %get-tuple-element.5), channel_id=1, replica_groups=mesh['req'=8,'kv'=32] {'kv'}, use_global_device_ids=true, to_apply=%region_4.5 | all-reduce | flops 512 | bytes 4096 | tf_op jit(solution)/shard_map/psum | solution.py:36
  217.3 0.1 constant_dynamic-slice_fusion
  217.4 0.1 copy.12
  217.5 76.3 %all-reduce.2.cloned.1.call-done = f32[4,128,512]{2,0,1:T(4,128)} async-done(((f32[4,128,512]{2,0,1:T(4,128)}), f32[4,128,512]{2,0,1:T(4,128)}) %all-reduce.2.cloned.1.call-update) | async-done | bytes 1048592 | tf_op jit(solution)/shard_map/psum | solution.py:36
  293.8 1.6 fusion.12
  (7 shorter events, 0.0 us)
Async XLA Ops:
  6.5 1.1 copy-start
  6.5 287.3 %all-reduce.2.cloned.1.call-start = ((), (), s32[]{:S(2)}) async-start(), calls=%async_computation | async-start | bytes 2097152 | tf_op jit(solution)/shard_map/psum | solution.py:36
  61.4 8.5 %slice-start = ((s8[9437184]{0:T(1024)(128)(4,1)}), s8[4194304]{0:T(1024)(128)(4,1)S(1)}, s32[]{:S(2)}) async-start(s8[9437184]{0:T(1024)(128)(4,1)} %bitcast.9), calls=%async_computation.1 | async-start | bytes 8388608
  62.3 7.6 %slice-start.1 = ((s8[9437184]{0:T(1024)(128)(4,1)}), s8[4194304]{0:T(1024)(128)(4,1)S(1)}, s32[]{:S(2)}) async-start(s8[9437184]{0:T(1024)(128)(4,1)} %bitcast.9), calls=%async_computation.2 | async-start | bytes 8388608
  62.3 7.6 %slice-start.2 = ((s8[9437184]{0:T(1024)(128)(4,1)}), s8[1048576]{0:T(1024)(128)(4,1)S(1)}, s32[]{:S(2)}) async-start(s8[9437184]{0:T(1024)(128)(4,1)} %bitcast.9), calls=%async_computation.3 | async-start | bytes 2097152
  69.9 223.9 %copy-start.1 = (bf16[4,512,128]{2,1,0:T(8,128)(2,1)S(1)}, bf16[4,512,128]{2,1,0:T(8,128)(2,1)}, u32[]{:S(2)}) copy-start(bf16[4,512,128]{2,1,0:T(8,128)(2,1)} %param.11) | copy-start | bytes 1572868
Sparse Core Ops, SparseCore 0:
  147.7 146.0 all-reduce.1
where the time goes:
time: 302 us
  blocking collectives  195 us (65%)
  waiting for transfers between devices  76.4 us (25%)
  between operations  13.5 us (4%)
  matrix products  12.2 us (4%)
  other arithmetic  3.94 us (1%)
    psum x1, waiting for transfers between devices, local(): lax.psum((local_out * factor[:, :, None], local_sum * factor), 'kv')  76.3 us
    pmax x1, blocking collectives, local(): top_score = lax.pmax(top_local, 'kv')  72.3 us
    psum x1, blocking collectives, local(): lax.psum((local_out * factor[:, :, None], local_sum * factor), 'kv')  69.7 us
    all_gather x1, blocking collectives, local(): queries_all = lax.all_gather(query_full, 'kv', axis=1, tiled=True)  52.9 us
    dot_general x1, matrix products, local(): jnp.einsum('bhk,btk->bht', queries_all, cache, preferred_element_type=jnp...  6.31 us
  transfers between devices with their start and end apart: 1, of which 1 were waited for; matrix products, arithmetic and copies ran while one was open for 0% of the time, Pallas kernels for 0%

commit v1 on v0

--- a/solution.py
+++ b/solution.py
@@ -13,7 +13,9 @@
         jnp.bfloat16
     )
     query_full = jnp.concatenate([q_lat, q_rope], axis=2)
-    queries_all = lax.all_gather(query_full, "kv", axis=1, tiled=True)
+    queries_all = jnp.concatenate(
+        lax.all_to_all(jnp.stack([query_full] * lax.axis_size("kv")), "kv", 0, 0), axis=1
+    )
     scores = (
         jnp.einsum("bhk,btk->bht", queries_all, cache, preferred_element_type=jnp.float32)
         * score_scale

time: 302 us -> 280 us (0.927)
  blocking collectives: 195 us -> 141 us
  waiting for transfers between devices: 76.4 us -> 95.5 us
  starting transfers between devices: 0.01 us -> 11.4 us
    all_gather x1 -> x0, blocking collectives: 52.9 us -> none  [local(): queries_all = lax.all_gather(query_full, 'kv', axis=1, tiled=True)]
    all_to_all x0 -> x1, waiting for transfers between devices: none -> 19.4 us  [local(): lax.all_to_all(jnp.stack([query_full] * lax.axis_size('kv')), 'kv', 0, 0)]
    all_to_all x0 -> x1, starting transfers between devices: none -> 11.3 us  [local(): lax.all_to_all(jnp.stack([query_full] * lax.axis_size('kv')), 'kv', 0, 0)]
  transfers between devices with their start and end apart: 1 -> 2, of which waited for: 1 -> 2; matrix products, arithmetic and copies ran while one was open for 0% -> 0% of each run, Pallas kernels for 0% -> 0%
where the time goes in v1:
time: 280 us
  blocking collectives  141 us (50%)
  waiting for transfers between devices  95.5 us (34%)
  between operations  13.5 us (5%)
  matrix products  12 us (4%)
  starting transfers between devices  11.4 us (4%)
  other arithmetic  3.79 us (1%)
    psum x1, waiting for transfers between devices, local(): lax.psum((local_out * factor[:, :, None], local_sum * factor), 'kv')  76.1 us
    pmax x1, blocking collectives, local(): top_score = lax.pmax(top_local, 'kv')  70.9 us
    psum x1, blocking collectives, local(): lax.psum((local_out * factor[:, :, None], local_sum * factor), 'kv')  70.4 us
    all_to_all x1, waiting for transfers between devices, local(): lax.all_to_all(jnp.stack([query_full] * lax.axis_size('kv')), 'kv', 0, 0)  19.4 us
    all_to_all x1, starting transfers between devices, local(): lax.all_to_all(jnp.stack([query_full] * lax.axis_size('kv')), 'kv', 0, 0)  11.3 us
    dot_general x1, matrix products, local(): jnp.einsum('bhk,btk->bht', queries_all, cache, preferred_element_type=jnp...  6.08 us
  transfers between devices with their start and end apart: 2, of which 2 were waited for; matrix products, arithmetic and copies ran while one was open for 0% of the time, Pallas kernels for 0%

profile of v1, /device:TPU:8, one launch (start us, length us, event | category | flops | bytes accessed | tf_op | source)
XLA Modules:
  0.0 279.8 jit_solution(10577536133569896030)
XLA Ops:
  6.5 0.0 copy-start
  6.5 0.7 copy.13
  7.3 0.3 copy-done
  7.6 0.9 fusion.11
  8.5 1.0 stack.2
  9.5 11.3 %all-to-all-start = ((bf16[32,4,4,576]{3,1,2,0:T(4,128)(2,1)}), bf16[32,4,4,576]{3,1,2,0:T(4,128)(2,1)S(1)}, u32[]{:S(2)}, u32[]{:S(2)}) async-start(bf16[32,4,4,576]{3,1,2,0:T(4,128)(2,1)} %stack.2), calls=%async_computation | async-start | bytes 1310720 | tf_op jit(solution)/shard_map/all_to_all | solution.py:17
  20.8 0.0 all-reduce.2.cloned.1.call-start
  20.9 0.7 broadcast_compare_fusion
  21.6 19.4 %all-to-all-done = bf16[32,4,4,576]{3,1,2,0:T(4,128)(2,1)S(1)} async-done(((bf16[32,4,4,576]{3,1,2,0:T(4,128)(2,1)}), bf16[32,4,4,576]{3,1,2,0:T(4,128)(2,1)S(1)}, u32[]{:S(2)}, u32[]{:S(2)}) %all-to-all-start) | async-done | bytes 589856 | tf_op jit(solution)/shard_map/all_to_all | solution.py:17
  41.0 6.1 %fusion.2 = (f32[4,128]{1,0:T(4,128)S(1)}, f32[4,128,2048]{2,1,0:T(8,128)S(1)}) fusion(pred[4,2048]{1,0:T(4,128)(4,1)S(1)} %broadcast_compare_fusion, bf16[4,2048,576]{1,2,0:T(8,128)(2,1)} %param.8, bf16[4,128,576]{2,0,1:T(4,128)(2,1)S(1)} %bitcast.14), kind=kOutput, calls=%fused_computation.4 | convolution fusion | flops 1211104768 | bytes 14231552 | tf_op jit(solution)/shard_map/bhk,btk->bht/dot_general | solution.py:20
  47.1 1.2 fusion.3
  48.4 0.0 slice-done
  48.4 0.0 copy-start.1
  48.4 3.4 %fusion = f32[4,128,512]{2,1,0:T(8,128)S(1)} fusion(bf16[4,2048,576]{1,2,0:T(8,128)(2,1)S(1)} %bitcast.13, f32[4,128,2048]{2,1,0:T(8,128)S(1)} %get-tuple-element.8, f32[4,128]{1,0:T(4,128)S(1)} %get-tuple-element.7, pred[4,2048]{1,0:T(4,128)(4,1)S(1)} %broadcast_compare_fusion), kind=kOutput, calls=%fused_computation | convolution fusion | flops 1078984704 | bytes 13641728 | tf_op jit(solution)/shard_map/bht,btc->bhc/dot_general | solution.py:29
  51.8 70.9 %pmax.7 = f32[4,128]{1,0:T(4,128)S(1)} all-reduce(f32[4,128]{1,0:T(4,128)S(1)} %get-tuple-element.7), channel_id=1, replica_groups=mesh['req'=8,'kv'=32] {'kv'}, use_global_device_ids=true, to_apply=%region_1.2 | all-reduce | flops 512 | bytes 4096 | tf_op jit(solution)/shard_map/pmax | solution.py:36
  122.7 0.1 copy.15
  122.8 1.8 copy_multiply_fusion
  124.6 0.0 all-reduce.2.cloned.1.call-update
  124.6 70.4 %psum.15 = f32[4,128]{1,0:T(4,128)S(1)} all-reduce(f32[4,128]{1,0:T(4,128)S(1)} %get-tuple-element.5), channel_id=1, replica_groups=mesh['req'=8,'kv'=32] {'kv'}, use_global_device_ids=true, to_apply=%region_4.5 | all-reduce | flops 512 | bytes 4096 | tf_op jit(solution)/shard_map/psum | solution.py:38
  195.1 0.1 constant_dynamic-slice_fusion
  195.2 0.1 copy.16
  195.2 76.1 %all-reduce.2.cloned.1.call-done = f32[4,128,512]{2,0,1:T(4,128)} async-done(((f32[4,128,512]{2,0,1:T(4,128)}), f32[4,128,512]{2,0,1:T(4,128)}) %all-reduce.2.cloned.1.call-update) | async-done | bytes 1048592 | tf_op jit(solution)/shard_map/psum | solution.py:38
  271.4 0.0 copy-done.1
  271.4 1.6 fusion.12
  (9 shorter events, 0.0 us)
Async XLA Ops:
  6.5 1.1 copy-start
  9.5 31.5 %all-to-all-start = ((bf16[32,4,4,576]{3,1,2,0:T(4,128)(2,1)}), bf16[32,4,4,576]{3,1,2,0:T(4,128)(2,1)S(1)}, u32[]{:S(2)}, u32[]{:S(2)}) async-start(bf16[32,4,4,576]{3,1,2,0:T(4,128)(2,1)} %stack.2), calls=%async_computation | async-start | bytes 1310720 | tf_op jit(solution)/shard_map/all_to_all | solution.py:17
  20.8 250.6 %all-reduce.2.cloned.1.call-start = ((), (), s32[]{:S(2)}) async-start(), calls=%async_computation.1 | async-start | bytes 2097152 | tf_op jit(solution)/shard_map/psum | solution.py:38
  41.0 7.3 %slice-start = ((s8[9437184]{0:T(1024)(128)(4,1)}), s8[4194304]{0:T(1024)(128)(4,1)S(1)}, s32[]{:S(2)}) async-start(s8[9437184]{0:T(1024)(128)(4,1)} %bitcast.12), calls=%async_computation.2 | async-start | bytes 8388608
  41.0 7.3 %slice-start.1 = ((s8[9437184]{0:T(1024)(128)(4,1)}), s8[4194304]{0:T(1024)(128)(4,1)S(1)}, s32[]{:S(2)}) async-start(s8[9437184]{0:T(1024)(128)(4,1)} %bitcast.12), calls=%async_computation.3 | async-start | bytes 8388608
  41.0 7.3 %slice-start.2 = ((s8[9437184]{0:T(1024)(128)(4,1)}), s8[1048576]{0:T(1024)(128)(4,1)S(1)}, s32[]{:S(2)}) async-start(s8[9437184]{0:T(1024)(128)(4,1)} %bitcast.12), calls=%async_computation.4 | async-start | bytes 2097152
  48.4 223.0 %copy-start.1 = (bf16[4,512,128]{2,1,0:T(8,128)(2,1)S(1)}, bf16[4,512,128]{2,1,0:T(8,128)(2,1)}, u32[]{:S(2)}) copy-start(bf16[4,512,128]{2,1,0:T(8,128)(2,1)} %param.11) | copy-start | bytes 1572868
Sparse Core Ops, SparseCore 0:
  124.8 146.5 all-reduce.1
